TPU v7x, 512 devices: a whole 4x4x16 slice. The times are simulated.
512 devices in a mesh: freq: 64 (over x, z_lo, core), tm: 4 (over y), tile: 2 (over z_hi).
Axes of the slice: x: 4, y: 4, z: 16 (z_hi: 2, z_lo: 8; z = z_hi * 8 + z_lo), core: 2. Of those that a mesh axis runs over, the one named last changes fastest.
Arguments:
- samples: bfloat16 [2048, 32, 2048], P('freq', ('tm', 'tile'))
- prototype: float32 [4, 2048], replicated, may hold values from -3 to 3
- feed_map: int32 [2048], replicated, may hold values from 0 to 2047, each once
- keep_mask: int32 [2048], replicated, may hold values 0 or 1
- tile_pairs: int32 [16, 2], replicated, may hold values from 0 to 31, as said below
Outputs:
- visibilities: float32 [16, 1024, 64, 128], P(('tm', 'tile'), 'freq')
Inputs may be any that keep to these rules, and one draw needn't show every extreme that they name: `tile_pairs`: each row is a pair of tile numbers below 32 with the first not above the second; no two rows are equal; every tile number appears in some row.
All inputs are finite; a program needn't handle non-finite values.
Results may differ from a plain program's by a relative error of at most 0.012.
Values may be sent and summed in bfloat16 or wider, within the bound.
A program may use at most 64 MiB of HBM per device.

v0:
```python
import math

import jax
import jax.numpy as jnp
from jax import lax
from jax.sharding import PartitionSpec as P

B = 64


def from_behind(value, axis, by):
    length = lax.axis_size(axis)
    pairs = [(i, i + by) for i in range(length) if 0 <= i + by < length]
    return lax.ppermute(value, axis, pairs)


def dft_table(points):
    rows = lax.broadcasted_iota(jnp.int32, (points, points), 0)
    columns = lax.broadcasted_iota(jnp.int32, (points, points), 1)
    phase = rows * (columns // 2) % points
    angle = phase.astype(jnp.float32) * (2.0 * math.pi / points)
    scale = 1.0 / math.sqrt(points)
    value = jnp.where(columns % 2 == 0, jnp.cos(angle), -jnp.sin(angle)) * scale
    return value.astype(jnp.bfloat16)


def cross_tiles(left_side, right_side, form, feed_dim):
    turned = jnp.stack([-right_side[..., 1], right_side[..., 0]], axis=-1)
    doubled = jnp.concatenate([right_side, turned], axis=feed_dim)
    return jnp.einsum(form, left_side, doubled, preferred_element_type=jnp.float32)


def mask_weight(keep_mask, row_feeds, col_feeds):
    weight = (
        keep_mask[row_feeds].astype(jnp.float32)[:, :, None]
        * keep_mask[col_feeds].astype(jnp.float32)[:, None, :]
    )
    return jnp.concatenate([weight, weight], axis=-1)


def shards(samples, prototype, feed_map, keep_mask, tile_pairs):
    taps = prototype.shape[0]
    inputs_local, frames_local, points = samples.shape
    groups = lax.axis_size("freq")
    nodes = lax.axis_size(("tm", "tile"))
    per_group = points // 2 // groups
    leading = from_behind(samples[:, frames_local - (taps - 1) :, :], ("tm", "tile"), 1)
    extended = jnp.concatenate([leading, samples], axis=1)
    total = jnp.zeros(samples.shape, jnp.float32)
    for lag in range(taps):
        total = total + prototype[lag] * extended[
            :, taps - 1 - lag : taps - 1 - lag + frames_local
        ].astype(jnp.float32)
    filtered = total.astype(jnp.bfloat16)
    spectra = jnp.dot(
        filtered.reshape(-1, points), dft_table(points), preferred_element_type=jnp.float32
    )
    spectra = spectra.astype(jnp.bfloat16)
    outgoing = spectra.reshape(inputs_local, frames_local, groups, 2 * per_group).transpose(
        2, 0, 1, 3
    )
    outgoing = outgoing.reshape(groups * inputs_local, frames_local * 2 * per_group)
    voltages = lax.all_to_all(outgoing, "freq", split_axis=0, concat_axis=0, tiled=True)
    total_inputs = voltages.shape[0]
    offsets = jnp.arange(B, dtype=jnp.int32)
    field = voltages.reshape(total_inputs, frames_local, per_group, 2)
    row_feeds = feed_map[tile_pairs[:, 0:1] * B + offsets]
    col_feeds = feed_map[tile_pairs[:, 1:2] * B + offsets]
    product = cross_tiles(field[row_feeds], field[col_feeds], "nafcp,nbfcp->ncab", 1)
    summed = lax.psum_scatter(
        (product * mask_weight(keep_mask, row_feeds, col_feeds)[:, None]).astype(jnp.bfloat16),
        ("tm", "tile"),
        scatter_dimension=0,
        tiled=True,
    ).astype(jnp.float32)
    return summed / (frames_local * nodes)


def solution(mesh):
    placed = (P("freq", ("tm", "tile"), None), P(), P(), P(), P())
    return jax.shard_map(
        shards,
        mesh=mesh,
        in_specs=placed,
        out_specs=P(("tm", "tile"), "freq", None, None),
        check_vma=False,
    )
```

profile of v0, /device:TPU:1, one launch (start us, length us, event | category | flops | bytes accessed | tf_op | source)
XLA Modules:
  0.0 442.1 jit_solution(3466708244959856550)
XLA Ops:
  6.5 1.4 slice.38
  7.9 16.3 %collective-permute-start = (bf16[32,3,2048]{2,1,0:T(4,128)(2,1)S(1)}, bf16[32,3,2048]{2,1,0:T(4,128)(2,1)S(1)}, u32[]{:S(2)}, u32[]{:S(2)}) collective-permute-start(bf16[32,3,2048]{2,1,0:T(4,128)(2,1)S(1)} %slice.38), channel_id=1, source_target_pairs={{0,1},{1,2},{2,3},{3,4},{4,5},{5,6},{6,7},{8,9},{9,10},{10,11},{11... | collective-permute-start | bytes 1179656 | tf_op jit(solution)/shard_map/ppermute | solution.py:14
  24.3 0.9 fusion.27
  25.2 14.0 %collective-permute-done = bf16[32,3,2048]{2,1,0:T(4,128)(2,1)S(1)} collective-permute-done((bf16[32,3,2048]{2,1,0:T(4,128)(2,1)S(1)}, bf16[32,3,2048]{2,1,0:T(4,128)(2,1)S(1)}, u32[]{:S(2)}, u32[]{:S(2)}) %collective-permute-start) | collective-permute-done | bytes 393248 | tf_op jit(solution)/shard_map/ppermute | solution.py:14
  39.2 3.9 add_convert_fusion
  43.1 0.1 reshape.135
  43.2 68.7 %fusion.7 = bf16[128,2048]{1,0:T(8,128)(2,1)S(1)} fusion(bf16[128,2048]{1,0:T(8,128)(2,1)S(1)} %reshape.135, s32[2048]{0:T(1024)S(1)} %get-tuple-element.13, s32[2048]{0:T(1024)S(1)} %get-tuple-element.16, s32[2048]{0:T(1024)S(1)} %get-tuple-element.14, s32[2048]{0:T(1024)S(1)} %get-tuple-element.15, pred[2048]{0:T(1024)(128)(4,1)S(1)} %get-tuple-element.17, ...), kind=kOutput, calls=%fused_computation.19 | convolution fusion | flops 1162084352 | bytes 1085440 | tf_op jit(solution)/shard_map/dot_general | solution.py:55
  112.0 1.6 reshape.136
  113.6 0.9 copy.24
  114.6 1.7 copy.25
  116.3 38.4 %all-to-all-start = ((bf16[64,32,128]{2,1,0:T(8,128)(2,1)}), bf16[64,32,128]{2,1,0:T(8,128)(2,1)S(1)}, u32[]{:S(2)}, u32[]{:S(2)}) async-start(bf16[64,32,128]{2,1,0:T(8,128)(2,1)} %copy.25), calls=%async_computation | async-start | bytes 1048576 | tf_op jit(solution)/shard_map/all_to_all | solution.py:63
  154.7 0.1 compare_select_fusion.1
  154.9 6.4 %gather_fusion.2 = s32[1024]{0:T(1024)S(1)} fusion(s32[2048]{0:T(1024)S(1)} %copy-done, s32[1024]{0:T(1024)S(1)} %broadcast_clamp_fusion), kind=kCustom, calls=%fused_computation.2 | custom fusion | bytes 12288 | tf_op jit(solution)/shard_map/gather | solution.py:68
  161.3 0.1 reshape.164
  161.4 6.1 %gather_fusion.5 = s32[1024]{0:T(1024)S(1)} fusion(s32[2048]{0:T(1024)S(1)} %copy-done.1, s32[1024]{0:T(1024)S(1)} %broadcast_clamp_fusion.1), kind=kCustom, calls=%fused_computation.5 | custom fusion | bytes 12288 | tf_op jit(solution)/shard_map/gather | solution.py:36
  167.7 6.1 %gather_fusion = s32[1024]{0:T(1024)S(1)} fusion(s32[2048]{0:T(1024)S(1)} %copy-done, s32[1024]{0:T(1024)S(1)} %broadcast_clamp_fusion.2), kind=kCustom, calls=%fused_computation | custom fusion | bytes 12288 | tf_op jit(solution)/shard_map/gather | solution.py:67
  173.9 0.1 reshape.148
  174.0 6.1 %gather_fusion.4 = s32[1024]{0:T(1024)S(1)} fusion(s32[2048]{0:T(1024)S(1)} %copy-done.1, s32[1024]{0:T(1024)S(1)} %broadcast_clamp_fusion.3), kind=kCustom, calls=%fused_computation.4 | custom fusion | bytes 12288 | tf_op jit(solution)/shard_map/gather | solution.py:35
  180.3 0.2 broadcast_multiply_fusion
  180.5 0.2 pad_maximum_fusion.1
  180.7 3.6 all-to-all-done
  184.2 3.0 copy.26
  187.2 2.1 reshape.137
  189.3 4.8 %copy.27 = bf16[2048,4,16,2]{2,1,3,0:T(4,128)(2,1)} copy(bf16[2048,4,16,2]{0,3,2,1:T(2,128)(2,1)S(1)} %reshape.137) | data formatting | bytes 1048576 | tf_op jit(solution)/shard_map/reshape | solution.py:66
  194.1 6.4 %gather_fusion.1 = bf16[1024,4,16,2]{2,1,3,0:T(4,128)(2,1)S(1)} fusion(bf16[2048,4,16,2]{2,1,3,0:T(4,128)(2,1)} %copy.27, s32[1024]{0:T(1024)S(1)} %broadcast_clamp_fusion.3), kind=kCustom, calls=%fused_computation.1 | custom fusion | bytes 528384 | tf_op jit(solution)/shard_map/gather | solution.py:69
  200.6 10.8 %gather_fusion.3 = bf16[1024,4,16,2]{2,1,3,0:T(4,128)(2,1)} fusion(bf16[2048,4,16,2]{2,1,3,0:T(4,128)(2,1)} %copy.27, s32[1024]{0:T(1024)S(1)} %broadcast_clamp_fusion.1), kind=kCustom, calls=%fused_computation.3 | custom fusion | bytes 528384 | tf_op jit(solution)/shard_map/gather | solution.py:69
  211.3 1.4 copy.34
  212.8 3.2 copy.33
  216.0 0.2 slice_negate_fusion
  216.2 4.3 fusion.3
  220.4 212.7 %reduce-scatter.2.cloned.1.call-done = bf16[2,16,64,128]{3,2,1,0:T(8,128)(2,1)} async-done(((bf16[16,16,64,128]{3,2,1,0:T(8,128)(2,1)}), bf16[2,16,64,128]{3,2,1,0:T(8,128)(2,1)}) %reduce-scatter.2.cloned.1.call-update) | async-done | bytes 524304 | tf_op jit(solution)/shard_map/reduce_scatter | solution.py:70
  433.2 2.1 convert_multiply_fusion
  (26 shorter events, 0.6 us)
Async XLA Ops:
  6.5 148.3 %copy-start = (s32[2048]{0:T(1024)S(1)}, s32[2048]{0:T(1024)}, u32[]{:S(2)}) copy-start(s32[2048]{0:T(1024)} %param.7) | copy-start | bytes 24580
  7.9 31.3 %collective-permute-start = (bf16[32,3,2048]{2,1,0:T(4,128)(2,1)S(1)}, bf16[32,3,2048]{2,1,0:T(4,128)(2,1)S(1)}, u32[]{:S(2)}, u32[]{:S(2)}) collective-permute-start(bf16[32,3,2048]{2,1,0:T(4,128)(2,1)S(1)} %slice.38), channel_id=1, source_target_pairs={{0,1},{1,2},{2,3},{3,4},{4,5},{5,6},{6,7},{8,9},{9,10},{10,11},{11... | collective-permute-start | bytes 1179656 | tf_op jit(solution)/shard_map/ppermute | solution.py:14
  112.0 42.7 %copy-start.2 = (s32[16,2]{0,1:T(2,128)S(1)}, s32[16,2]{0,1:T(2,128)}, u32[]{:S(2)}) copy-start(s32[16,2]{0,1:T(2,128)} %param.9) | copy-start | bytes 388
  116.3 68.0 %all-to-all-start = ((bf16[64,32,128]{2,1,0:T(8,128)(2,1)}), bf16[64,32,128]{2,1,0:T(8,128)(2,1)S(1)}, u32[]{:S(2)}, u32[]{:S(2)}) async-start(bf16[64,32,128]{2,1,0:T(8,128)(2,1)} %copy.25), calls=%async_computation | async-start | bytes 1048576 | tf_op jit(solution)/shard_map/all_to_all | solution.py:63
  154.6 278.5 %reduce-scatter.2.cloned.1.call-start = ((), (), s32[]{:S(2)}) async-start(), calls=%async_computation.2 | async-start | bytes 4718592 | tf_op jit(solution)/shard_map/reduce_scatter | solution.py:70
  154.9 6.5 %copy-start.1 = (s32[2048]{0:T(1024)S(1)}, s32[2048]{0:T(1024)}, u32[]{:S(2)}) copy-start(s32[2048]{0:T(1024)} %param.8) | copy-start | bytes 24580
Sparse Core Ops, SparseCore 0:
  220.6 212.5 reduce-scatter.1
where the time goes:
time: 443 us; the launch traced here: 442 us
  waiting for transfers between devices  230 us (52%)
  matrix products  73 us (16%)
  local copies, waits for them, and re-layouts  63.8 us (14%)
  starting transfers between devices  54.7 us (12%)
  between operations  13.6 us (3%)
  other arithmetic  6.72 us (2%)
    reduce_scatter x1, waiting for transfers between devices, shards(): lax.psum_scatter((product * mask_weight(keep_mask, row_feeds, col_feeds)[...  213 us
    dot_general x1, matrix products, shards(): jnp.dot(filtered.reshape(-1, points), dft_table(points), preferred_elemen...  68.7 us
    all_to_all x1, starting transfers between devices, shards(): lax.all_to_all(outgoing, 'freq', split_axis=0, concat_axis=0, tiled=True)  38.4 us
    ppermute x1, starting transfers between devices, from_behind(): return lax.ppermute(value, axis, pairs)  16.3 us
    ppermute x1, waiting for transfers between devices, from_behind(): return lax.ppermute(value, axis, pairs)  14 us
    gather x2, local copies, waits for them, and re-layouts, shards(): field[col_feeds]  14 us
  transfers between devices with their start and end apart: 3, of which 3 were waited for; matrix products, arithmetic and copies ran while one was open for 6% of the time, Pallas kernels for 0%

commit v1 on v0

v1 whole, which is shorter than its diff:
```python
import math

import jax
import jax.numpy as jnp
import numpy as np
from jax import lax
from jax.sharding import PartitionSpec as P

B = 64


def from_behind(value, axis, by):
    length = lax.axis_size(axis)
    pairs = [(i, i + by) for i in range(length) if 0 <= i + by < length]
    return lax.ppermute(value, axis, pairs)


def dft_table(points):
    rows = np.arange(points)[:, None]
    columns = np.arange(points)[None, :]
    angle = (rows * (columns // 2) % points) * (2.0 * math.pi / points)
    value = np.where(columns % 2 == 0, np.cos(angle), -np.sin(angle)) / math.sqrt(points)
    return jnp.asarray(value.astype(np.float32)).astype(jnp.bfloat16)


def shards(samples, prototype, feed_map, keep_mask, tile_pairs):
    taps = prototype.shape[0]
    inputs_local, frames_local, points = samples.shape
    groups = lax.axis_size("freq")
    nodes = lax.axis_size(("tm", "tile"))
    per_group = points // 2 // groups
    total_inputs = inputs_local * groups
    leading = from_behind(samples[:, frames_local - (taps - 1) :, :], ("tm", "tile"), 1)
    extended = jnp.concatenate([leading, samples], axis=1)
    total = jnp.zeros(samples.shape, jnp.float32)
    for lag in range(taps):
        total = total + prototype[lag] * extended[
            :, taps - 1 - lag : taps - 1 - lag + frames_local
        ].astype(jnp.float32)
    filtered = total.astype(jnp.bfloat16)
    spectra = jnp.dot(
        filtered.reshape(-1, points), dft_table(points), preferred_element_type=jnp.float32
    )
    spectra = spectra.astype(jnp.bfloat16)
    outgoing = spectra.reshape(inputs_local, frames_local, groups, 2 * per_group).transpose(
        2, 0, 1, 3
    )
    outgoing = outgoing.reshape(groups * inputs_local, frames_local * 2 * per_group)
    voltages = lax.all_to_all(outgoing, "freq", split_axis=0, concat_axis=0, tiled=True)

    sides = tile_pairs.reshape(-1)
    hit = sides[:, None] == jnp.arange(total_inputs // B, dtype=jnp.int32)[None, :]
    feeds = jnp.sum(
        jnp.where(hit[:, :, None], feed_map.reshape(1, -1, B), 0), axis=1
    ).reshape(-1)
    place = jnp.where(
        feeds[:, None] == jnp.arange(total_inputs, dtype=jnp.int32)[None, :],
        keep_mask[None, :],
        0,
    ).astype(jnp.bfloat16)
    ordered = jnp.dot(place, voltages, preferred_element_type=jnp.float32).astype(jnp.bfloat16)
    field = lax.all_to_all(ordered, ("tm", "tile"), split_axis=0, concat_axis=0, tiled=True)
    tiles = tile_pairs.shape[0] // nodes
    field = field.reshape(nodes, tiles, 2, B, frames_local, per_group, 2)
    left, right = field[:, :, 0], field[:, :, 1]
    turned = jnp.stack([-right[..., 1], right[..., 0]], axis=-1)
    doubled = jnp.concatenate([right, turned], axis=2)
    product = jnp.einsum(
        "ntafcp,ntbfcp->tcab", left, doubled, preferred_element_type=jnp.float32
    )
    return product / (frames_local * nodes)


def solution(mesh):
    placed = (P("freq", ("tm", "tile"), None), P(), P(), P(), P())
    return jax.shard_map(
        shards,
        mesh=mesh,
        in_specs=placed,
        out_specs=P(("tm", "tile"), "freq", None, None),
        check_vma=False,
    )
```

time: 443 us -> 170 us (0.38)
  the two profiles are of different devices: /device:TPU:1 before, /device:TPU:35 now
where the time goes in v1:
time: 170 us; the launch traced here: 169 us
  waiting for transfers between devices  64.1 us (38%)
  blocking collectives  50.2 us (30%)
  starting transfers between devices  31.1 us (18%)
  local copies, waits for them, and re-layouts  10.4 us (6%)
  matrix products  9.14 us (5%)
  other arithmetic  4.18 us (2%)
    all_to_all x1, blocking collectives, shards(): lax.all_to_all(ordered, ('tm', 'tile'), split_axis=0, concat_axis=0, tile...  50.2 us
    ppermute x1, waiting for transfers between devices, from_behind(): return lax.ppermute(value, axis, pairs)  36.6 us
    all_to_all x1, waiting for transfers between devices, shards(): lax.all_to_all(outgoing, 'freq', split_axis=0, concat_axis=0, tiled=True)  27.5 us
    all_to_all x1, starting transfers between devices, shards(): lax.all_to_all(outgoing, 'freq', split_axis=0, concat_axis=0, tiled=True)  16.5 us
    ppermute x1, starting transfers between devices, from_behind(): return lax.ppermute(value, axis, pairs)  14.6 us
    dot_general x1, matrix products, shards(): jnp.dot(filtered.reshape(-1, points), dft_table(points), preferred_elemen...  4.65 us
    convert_element_type x1, other arithmetic, shards(): filtered = total.astype(jnp.bfloat16)  3.81 us
  transfers between devices with their start and end apart: 2, of which 2 were waited for; matrix products, arithmetic and copies ran while one was open for 1% of the time, Pallas kernels for 0%

profile of v1, /device:TPU:35, one launch (start us, length us, event | category | flops | bytes accessed | tf_op | source)
XLA Modules:
  0.0 169.2 jit_solution(9450540885845379613)
XLA Ops:
  0.0 1.4 slice.38
  1.4 14.6 %collective-permute-start = (bf16[32,3,2048]{2,1,0:T(4,128)(2,1)S(1)}, bf16[32,3,2048]{2,1,0:T(4,128)(2,1)S(1)}, u32[]{:S(2)}, u32[]{:S(2)}) collective-permute-start(bf16[32,3,2048]{2,1,0:T(4,128)(2,1)S(1)} %slice.38), channel_id=1, source_target_pairs={{0,1},{1,2},{2,3},{3,4},{4,5},{5,6},{6,7},{8,9},{9,10},{10,11},{11... | collective-permute-start | bytes 1179656 | tf_op jit(solution)/shard_map/ppermute | solution.py:15
  15.9 0.9 fusion.16
  16.9 36.6 %collective-permute-done = bf16[32,3,2048]{2,1,0:T(4,128)(2,1)S(1)} collective-permute-done((bf16[32,3,2048]{2,1,0:T(4,128)(2,1)S(1)}, bf16[32,3,2048]{2,1,0:T(4,128)(2,1)S(1)}, u32[]{:S(2)}, u32[]{:S(2)}) %collective-permute-start) | collective-permute-done | bytes 393248 | tf_op jit(solution)/shard_map/ppermute | solution.py:15
  53.4 3.8 %add_convert_fusion = bf16[32,4,2048]{2,1,0:T(4,128)(2,1)S(1)} fusion(bf16[32,4,2048]{2,1,0:T(4,128)(2,1)} %param.6, bf16[32,3,2048]{2,1,0:T(4,128)(2,1)S(1)} %collective-permute-done, f32[2048]{0:T(1024)S(1)} %bitcast.33, f32[2048]{0:T(1024)S(1)} %bitcast.34, f32[2048]{0:T(1024)S(1)} %bitcast.32, f32[2048]{0:T(1024)S(1)} %bitcast.31), kind=kLoop, calls=%fused_computation.14 | loop fusion | flops 5505024 | bytes 1474560 | tf_op jit(solution)/shard_map/convert_element_type | solution.py:40
  57.3 0.1 reshape.48
  57.4 0.0 copy-start
  57.4 0.0 copy-start.1
  57.4 0.0 copy-start.2
  57.4 4.6 %convolution_convert_fusion = bf16[128,2048]{1,0:T(8,128)(2,1)S(1)} fusion(bf16[128,2048]{1,0:T(8,128)(2,1)S(1)} %reshape.48, bf16[2048,2048]{1,0:T(8,128)(2,1)} %constant.9), kind=kOutput, calls=%fused_computation.6 | convolution fusion | flops 1074003968 | bytes 9437184 | tf_op jit(solution)/shard_map/dot_general | solution.py:41
  62.1 1.6 reshape.49
  63.7 0.9 copy.26
  64.7 1.6 copy.27
  66.3 16.5 %all-to-all-start = ((bf16[64,32,128]{2,1,0:T(8,128)(2,1)}), bf16[64,32,128]{2,1,0:T(8,128)(2,1)S(1)}, u32[]{:S(2)}, u32[]{:S(2)}) async-start(bf16[64,32,128]{2,1,0:T(8,128)(2,1)} %copy.27), calls=%async_computation | async-start | bytes 1048576 | tf_op jit(solution)/shard_map/all_to_all | solution.py:49
  82.8 0.0 copy-done
  82.8 0.1 broadcast_in_dim.39
  82.9 0.0 copy-done.1
  82.9 0.1 copy.25
  83.0 0.1 eq.34
  83.1 0.1 iota_compare_fusion.1
  83.2 0.2 select_reduce_fusion
  83.4 0.1 eq.38
  83.5 27.5 %all-to-all-done = bf16[64,32,128]{2,1,0:T(8,128)(2,1)S(1)} async-done(((bf16[64,32,128]{2,1,0:T(8,128)(2,1)}), bf16[64,32,128]{2,1,0:T(8,128)(2,1)S(1)}, u32[]{:S(2)}, u32[]{:S(2)}) %all-to-all-start) | async-done | bytes 524320 | tf_op jit(solution)/shard_map/all_to_all | solution.py:49
  111.0 0.0 copy-done.2
  111.0 2.6 %fusion.4 = bf16[2048,128]{1,0:T(8,128)(2,1)S(1)} fusion(bf16[2048,128]{1,0:T(8,128)(2,1)S(1)} %bitcast.29, s32[2048]{0:T(1024)S(1)} %copy-done.2, s32[2048]{0:T(1024)S(1)} %eq.38), kind=kOutput, calls=%fused_computation.7 | convolution fusion | flops 1086586880 | bytes 1064960 | tf_op jit(solution)/shard_map/dot_general | solution.py:61
  113.6 0.2 copy.28
  113.8 50.2 %all_to_all.21 = bf16[8,256,128]{1,2,0:T(8,128)(2,1)S(1)} all-to-all(bf16[8,256,128]{1,2,0:T(8,128)(2,1)S(1)} %copy.28), channel_id=1, replica_groups=mesh['freq'=64,'tm'=4,'tile'=2] {'tm','tile'}, dimensions={0} | all-to-all | bytes 1048576 | tf_op jit(solution)/shard_map/all_to_all | solution.py:62
  164.0 0.4 reshape.50
  164.4 2.2 %fusion.15 = (bf16[8,2,1,64,4,16,2]{3,2,1,6,5,4,0:T(2,128)(2,1)S(1)}, bf16[8,2,1,64,4,16,2]{3,2,1,6,5,4,0:T(2,128)(2,1)S(1)}) fusion(bf16[8,2,2,64,4,16,2]{3,2,1,6,5,4,0:T(2,128)(2,1)S(1)} %reshape.50), kind=kLoop, calls=%fused_computation.30 | loop fusion | bytes 1048576 | tf_op jit(solution)/shard_map/slice | solution.py:65
  166.6 0.6 copy.37
  167.2 0.1 slice_negate_fusion
  167.3 1.9 %fusion.5 = f32[2,16,64,128]{3,2,1,0:T(8,128)} fusion(bf16[8,2,64,4,16,1]{2,0,5,3,4,1:T(8,128)(2,1)S(1)} %get-tuple-element.8, bf16[8,2,64,4,16,1]{2,0,5,3,4,1:T(8,128)(2,1)S(1)} %get-tuple-element.7, bf16[8,2,64,4,16,2]{2,0,5,3,4,1:T(8,128)(2,1)S(1)} %bitcast.28, bf16[8,2,1,64,4,16,2]{3,2,1,6,5,4,0:T(2,128)(2,1)S(1)} %get-tuple-element.5), kind=kOutput, calls=%fused_computation.9 | convolution fusion | flops 35389440 | bytes 1835008 | tf_op jit(solution)/shard_map/ntafcp,ntbfcp->tcab/dot_general | solution.py:68
Async XLA Ops:
  1.4 52.1 %collective-permute-start = (bf16[32,3,2048]{2,1,0:T(4,128)(2,1)S(1)}, bf16[32,3,2048]{2,1,0:T(4,128)(2,1)S(1)}, u32[]{:S(2)}, u32[]{:S(2)}) collective-permute-start(bf16[32,3,2048]{2,1,0:T(4,128)(2,1)S(1)} %slice.38), channel_id=1, source_target_pairs={{0,1},{1,2},{2,3},{3,4},{4,5},{5,6},{6,7},{8,9},{9,10},{10,11},{11... | collective-permute-start | bytes 1179656 | tf_op jit(solution)/shard_map/ppermute | solution.py:15
  57.4 25.4 %copy-start = (s32[2048]{0:T(1024)S(1)}, s32[2048]{0:T(1024)}, u32[]{:S(2)}) copy-start(s32[2048]{0:T(1024)} %param.8) | copy-start | bytes 24580
  57.4 25.5 %copy-start.1 = (s32[16,2]{0,1:T(2,128)S(1)}, s32[16,2]{0,1:T(2,128)}, u32[]{:S(2)}) copy-start(s32[16,2]{0,1:T(2,128)} %param.10) | copy-start | bytes 388
  57.4 53.6 %copy-start.2 = (s32[2048]{0:T(1024)S(1)}, s32[2048]{0:T(1024)}, u32[]{:S(2)}) copy-start(s32[2048]{0:T(1024)} %param.9) | copy-start | bytes 24580
  66.3 44.7 %all-to-all-start = ((bf16[64,32,128]{2,1,0:T(8,128)(2,1)}), bf16[64,32,128]{2,1,0:T(8,128)(2,1)S(1)}, u32[]{:S(2)}, u32[]{:S(2)}) async-start(bf16[64,32,128]{2,1,0:T(8,128)(2,1)} %copy.27), calls=%async_computation | async-start | bytes 1048576 | tf_op jit(solution)/shard_map/all_to_all | solution.py:49

commit v2 on v1

v2 whole, which is shorter than its diff:
```python
import math

import jax
import jax.numpy as jnp
import numpy as np
from jax import lax
from jax.experimental import pallas as pl
from jax.experimental.pallas import tpu as pltpu
from jax.sharding import PartitionSpec as P

MESH = pl.DeviceIdType.MESH
B = 64
HALF = 16
LANES = 128


def dft_table(points, groups):
    per_group = points // 2 // groups
    column = np.arange(points)
    group, rest = column // (2 * per_group), column % (2 * per_group)
    part, channel = rest // per_group, group * per_group + rest % per_group
    angle = (np.arange(points)[:, None] * channel[None, :] % points) * (2.0 * math.pi / points)
    value = np.where(part[None, :] == 0, np.cos(angle), -np.sin(angle)) / math.sqrt(points)
    return jnp.asarray(value.astype(np.float32)).astype(jnp.bfloat16)


def kernel(
    sizes,
    x_ref,
    proto_ref,
    table_hbm,
    feeds_ref,
    source_ref,
    keep_lane_ref,
    out_ref,
    table_ref,
    place_ref,
    halo_ref,
    filt_ref,
    turn_out,
    turn_in,
    cat_ref,
    tile_out,
    tile_in,
    left_ref,
    right_ref,
    table_sem,
    halo_send,
    halo_recv,
    turn_send,
    turn_recv,
    tile_send,
    tile_recv,
):
    groups, n_tm, n_tile = sizes
    nodes = n_tm * n_tile
    me, tm, tile = lax.axis_index("freq"), lax.axis_index("tm"), lax.axis_index("tile")
    node = tm * n_tile + tile
    frames, inputs, points = x_ref.shape

    def node_id(k):
        return (me, lax.div(k, n_tile), lax.rem(k, n_tile))

    table_copy = pltpu.make_async_copy(table_hbm, table_ref, table_sem)
    table_copy.start()

    barrier = pltpu.get_barrier_semaphore()

    def greet_group(k, carry):
        pl.semaphore_signal(
            barrier, 1, device_id=(lax.rem(me + k, groups), tm, tile), device_id_type=MESH
        )
        return carry

    def greet_node(k, carry):
        pl.semaphore_signal(
            barrier, 1, device_id=node_id(lax.rem(node + k, nodes)), device_id_type=MESH
        )
        return carry

    lax.fori_loop(1, nodes, greet_node, 0)
    lax.fori_loop(1, groups, greet_group, 0)
    pl.semaphore_wait(barrier, groups - 1 + nodes - 1)

    def halo_copy(j):
        return pltpu.make_async_remote_copy(
            src_ref=x_ref.at[j + 1],
            dst_ref=halo_ref.at[j],
            send_sem=halo_send.at[j],
            recv_sem=halo_recv.at[j],
            device_id=node_id(lax.rem(node + 1, nodes)),
            device_id_type=MESH,
        )

    taps = proto_ref.shape[0]

    @pl.when(node < nodes - 1)
    def _():
        for j in range(taps - 2, -1, -1):
            halo_copy(j).start()

    def build(k, carry):
        rows = pl.ds(pl.multiple_of(k * 128, 128), 128)
        hit = feeds_ref[rows, :] == source_ref[...]
        place_ref[rows, :] = jnp.where(hit, 1.0, 0.0).astype(jnp.bfloat16)
        return carry

    lax.fori_loop(0, place_ref.shape[0] // 128, build, 0)

    def wait_halo(j):
        @pl.when(node == 0)
        def _():
            halo_ref[j] = jnp.zeros(halo_ref.shape[1:], halo_ref.dtype)

        @pl.when(node > 0)
        def _():
            halo_copy(j).wait_recv()

    def filter_frame(j, row):
        def columns(q, carry):
            cols = pl.ds(pl.multiple_of(q * 512, 512), 512)
            total = None
            for lag in range(taps):
                k = j - lag
                frame = x_ref[k, :, cols] if k >= 0 else halo_ref[taps - 1 + k, :, cols]
                term = proto_ref[lag : lag + 1, cols] * frame.astype(jnp.float32)
                total = term if total is None else total + term
            filt_ref[row * inputs : (row + 1) * inputs, cols] = total.astype(jnp.bfloat16)
            return carry

        lax.fori_loop(0, points // 512, columns, 0)

    width = points // groups

    def channelize(chunk):
        def columns(q, carry):
            cols = pl.ds(pl.multiple_of(q * 256, 256), 256)
            y = jnp.dot(filt_ref[...], table_ref[:, cols], preferred_element_type=jnp.float32)
            for b in range(256 // width):
                pieces = [
                    y[f * inputs + i * HALF : f * inputs + (i + 1) * HALF, b * width : (b + 1) * width]
                    for i in range(2)
                    for f in range(2)
                ]
                turn_out[chunk, q * (256 // width) + b] = jnp.concatenate(pieces, axis=1).astype(
                    jnp.bfloat16
                )
            return carry

        lax.fori_loop(0, points // 256, columns, 0)

    def turn_copy(chunk, k):
        peer = lax.rem(me + k, groups)
        return pltpu.make_async_remote_copy(
            src_ref=turn_out.at[chunk, peer],
            dst_ref=turn_in.at[chunk, me],
            send_sem=turn_send.at[chunk],
            recv_sem=turn_recv.at[chunk],
            device_id=(peer, tm, tile),
            device_id_type=MESH,
        )

    def turn_all(chunk):
        return pltpu.make_async_remote_copy(
            src_ref=turn_out.at[chunk, pl.ds(0, groups - 1)],
            dst_ref=turn_in.at[chunk, pl.ds(0, groups - 1)],
            send_sem=turn_send.at[chunk],
            recv_sem=turn_recv.at[chunk],
            device_id=(lax.rem(me + 1, groups), tm, tile),
            device_id_type=MESH,
        )

    def send_turn(chunk):
        def go(k, carry):
            turn_copy(chunk, k).start()
            return carry

        lax.fori_loop(1, groups, go, 0)
        turn_in[chunk, me] = turn_out[chunk, me]

    def tile_copy(chunk, k):
        peer = lax.rem(node + k, nodes)
        return pltpu.make_async_remote_copy(
            src_ref=tile_out.at[chunk, peer],
            dst_ref=tile_in.at[chunk, node],
            send_sem=tile_send.at[chunk],
            recv_sem=tile_recv.at[chunk],
            device_id=node_id(peer),
            device_id_type=MESH,
        )

    def tile_all(chunk):
        return pltpu.make_async_remote_copy(
            src_ref=tile_out.at[chunk, pl.ds(0, nodes - 1)],
            dst_ref=tile_in.at[chunk, pl.ds(0, nodes - 1)],
            send_sem=tile_send.at[chunk],
            recv_sem=tile_recv.at[chunk],
            device_id=node_id(lax.rem(node + 1, nodes)),
            device_id_type=MESH,
        )

    rows_all = groups * HALF
    rows_node = tile_out.shape[2]
    per_step = 4

    def arrange(chunk):
        turn_all(chunk).wait_recv()
        block = turn_in[chunk].reshape(rows_all, LANES)
        turned = jnp.concatenate([block[:, B:], block[:, :B]], axis=1)
        cat_ref[0:rows_all] = block
        cat_ref[rows_all : 2 * rows_all] = turned
        low = lax.broadcasted_iota(jnp.int32, (per_step * rows_node, LANES), 1) < B

        def step(k, carry):
            size = per_step * rows_node
            first = pl.multiple_of(k * size, size)
            second = pl.multiple_of(nodes * rows_node + k * size, size)
            left = jnp.dot(
                place_ref[pl.ds(first, size), :], cat_ref[...], preferred_element_type=jnp.float32
            )
            right = jnp.dot(
                place_ref[pl.ds(second, size), :], cat_ref[...], preferred_element_type=jnp.float32
            )
            right = jnp.concatenate([right[:, B:], right[:, :B]], axis=1)
            both = jnp.where(low, left, right).astype(jnp.bfloat16)
            tile_out[chunk, pl.ds(k * per_step, per_step)] = both.reshape(
                per_step, rows_node, LANES
            )
            return carry

        lax.fori_loop(0, nodes // per_step, step, 0)

        def go(k, carry):
            tile_copy(chunk, k).start()
            return carry

        lax.fori_loop(1, nodes, go, 0)
        tile_in[chunk, node] = tile_out[chunk, node]

    filter_frame(3, 0)
    table_copy.wait()
    wait_halo(2)
    filter_frame(2, 1)
    channelize(0)
    send_turn(0)
    wait_halo(1)
    filter_frame(1, 0)
    wait_halo(0)
    filter_frame(0, 1)
    channelize(1)
    send_turn(1)
    arrange(0)
    arrange(1)

    tile_all(0).wait_recv()
    tile_all(1).wait_recv()
    lane = lax.broadcasted_iota(jnp.int32, (B, LANES), 1)
    low = lane < B
    channels = out_ref.shape[1]
    first_part = lax.rem(lane, 2 * channels) < channels
    for t in range(out_ref.shape[0]):
        for k in range(nodes):
            one = tile_in[0, k, t * B : (t + 1) * B, :].astype(jnp.float32)
            two = tile_in[1, k, t * B : (t + 1) * B, :].astype(jnp.float32)
            one_turned = pltpu.roll(one, B, 1)
            two_turned = pltpu.roll(two, B, 1)
            left = jnp.where(low, one, two_turned)
            right = jnp.where(low, one_turned, two)
            cross = jnp.where(
                first_part, -pltpu.roll(right, LANES - channels, 1), pltpu.roll(right, channels, 1)
            )
            cols = slice(k * LANES, (k + 1) * LANES)
            left_ref[:, cols] = left.astype(jnp.bfloat16)
            right_ref[0:B, cols] = right.astype(jnp.bfloat16)
            right_ref[B : 2 * B, cols] = cross.astype(jnp.bfloat16)
        masked = (left_ref[...][None] * keep_lane_ref[...][:, None, :]).reshape(
            channels * B, nodes * LANES
        )
        product = lax.dot_general(
            masked, right_ref[...], (((1,), (1,)), ((), ())), preferred_element_type=jnp.float32
        )
        out_ref[t] = (product * (1.0 / (frames * nodes))).reshape(channels, B, LANES)

    @pl.when(node < nodes - 1)
    def _():
        for j in range(taps - 2, -1, -1):
            halo_copy(j).wait_send()

    for chunk in range(2):
        turn_all(chunk).wait_send()
        tile_all(chunk).wait_send()


def solution(mesh):
    groups, n_tm, n_tile = mesh.shape["freq"], mesh.shape["tm"], mesh.shape["tile"]
    nodes = n_tm * n_tile

    def shards(samples, prototype, feed_map, keep_mask, tile_pairs):
        taps = prototype.shape[0]
        inputs, frames, points = samples.shape
        total = inputs * groups
        tiles = tile_pairs.shape[0] // nodes
        channels = points // 2 // groups
        sides = tile_pairs.T.reshape(-1)
        hit = sides[:, None] == jnp.arange(total // B, dtype=jnp.int32)[None, :]
        feeds = jnp.sum(
            jnp.where(hit[:, :, None], feed_map.reshape(1, -1, B), 0), axis=1
        ).reshape(-1, 1)
        source = jnp.where(keep_mask != 0, jnp.arange(total, dtype=jnp.int32), -1)
        source = source.reshape(groups, 2, HALF).transpose(1, 0, 2).reshape(1, total)
        lane = np.arange(nodes * LANES) % (B // 2)
        keep_lane = jnp.asarray(
            (lane[None, :] % channels == np.arange(channels)[:, None]).astype(np.float32)
        ).astype(jnp.bfloat16)
        vmem = pl.BlockSpec(memory_space=pltpu.VMEM)
        bf = jnp.bfloat16
        body = lambda *refs: kernel((groups, n_tm, n_tile), *refs)
        return pl.pallas_call(
            body,
            out_shape=jax.ShapeDtypeStruct((tiles, channels, B, 2 * B), jnp.float32),
            in_specs=[vmem, vmem, pl.BlockSpec(memory_space=pl.ANY), vmem, vmem, vmem],
            out_specs=vmem,
            scratch_shapes=[
                pltpu.VMEM((points, points), bf),
                pltpu.VMEM((total, total), bf),
                pltpu.VMEM((taps - 1, inputs, points), bf),
                pltpu.VMEM((2 * inputs, points), bf),
                pltpu.VMEM((2, groups, HALF, LANES), bf),
                pltpu.VMEM((2, groups, HALF, LANES), bf),
                pltpu.VMEM((2 * groups * HALF, LANES), bf),
                pltpu.VMEM((2, nodes, tiles * B, LANES), bf),
                pltpu.VMEM((2, nodes, tiles * B, LANES), bf),
                pltpu.VMEM((B, nodes * LANES), bf),
                pltpu.VMEM((2 * B, nodes * LANES), bf),
                pltpu.SemaphoreType.DMA,
                pltpu.SemaphoreType.DMA((taps - 1,)),
                pltpu.SemaphoreType.DMA((taps - 1,)),
                pltpu.SemaphoreType.DMA((2,)),
                pltpu.SemaphoreType.DMA((2,)),
                pltpu.SemaphoreType.DMA((2,)),
                pltpu.SemaphoreType.DMA((2,)),
            ],
            compiler_params=pltpu.CompilerParams(
                collective_id=0, has_side_effects=True, vmem_limit_bytes=48 * 2**20
            ),
            cost_estimate=pl.CostEstimate(flops=4 * 10**9, bytes_accessed=10**7, transcendentals=0),
        )(samples.transpose(1, 0, 2), prototype, dft_table(points, groups), feeds, source, keep_lane)

    return jax.shard_map(
        shards,
        mesh=mesh,
        in_specs=(P("freq", ("tm", "tile"), None), P(), P(), P(), P()),
        out_specs=P(("tm", "tile"), "freq", None, None),
        check_vma=False,
    )
```

time: 170 us -> 123 us (0.72)
  the two profiles are of different devices: /device:TPU:35 before, /device:TPU:1 now
where the time goes in v2:
time: 123 us; the launch traced here: 121 us
  Pallas kernels  113 us (92%)
  local copies, waits for them, and re-layouts  6.57 us (5%)
    pallas_call x1, Pallas kernels, shards(): pl.pallas_call(body, out_shape=jax.ShapeDtypeStruct((tiles, channels, B,...  113 us
    unnamed x6, local copies, waits for them, and re-layouts  3.82 us

profile of v2, /device:TPU:1, one launch (start us, length us, event | category | flops | bytes accessed | tf_op | source)
XLA Modules:
  0.0 120.8 jit_solution(7519850968868165992)
XLA Ops:
  0.0 0.8 eq.19
  0.8 0.1 iota_compare_fusion
  0.8 0.7 iota_select_fusion
  1.5 0.8 broadcast_in_dim.29
  2.3 0.2 select_reduce_fusion
  2.5 0.1 reshape.36
  2.7 0.1 reshape.37.refs_4_
  2.8 1.3 %copy.16 = bf16[32,4,2048]{2,0,1:T(8,128)(2,1)S(1)} copy(bf16[32,4,2048]{2,1,0:T(4,128)(2,1)} %param.7) | data formatting | bytes 1048576 | tf_op args[0]
  4.1 1.0 reshape.38.refs_3_
  5.1 0.0 copy-start
  5.1 0.8 copy-done
  5.9 0.0 copy-start.1
  5.9 0.8 copy-done.1
  6.6 113.2 %shard_map.73 = f32[2,16,64,128]{3,2,1,0:T(8,128)S(1)} custom-call(bf16[4,32,2048]{2,1,0:T(8,128)(2,1)S(1)} %bitcast.5, f32[4,2048]{1,0:T(4,128)S(1)} %copy-done, bf16[2048,2048]{1,0:T(8,128)(2,1)} %constant.12.refs_2_, s32[2048,1]{1,0:T(8,128)S(1)} %reshape.38.refs_3_, s32[1,2048]{1,0:T(1,128)S(1)} %reshape.37.refs_4_, bf16[16,1024]{1,0:T(8,128)(2,1)S(1)} %copy-done.1), custom_call_target="tpu_custom_call" | custom-call | flops 4000000000 | bytes 10000000 | tf_op jit(solution)/shard_map/pallas_call | solution.py:318
  119.9 1.0 copy.18
  (1 shorter events, 0.0 us)
Async XLA Ops:
  5.1 0.8 copy-start
  5.9 0.8 copy-start.1

commit v3 on v2

v3 whole, which is shorter than its diff:
```python
import math

import jax
import jax.numpy as jnp
import numpy as np
from jax import lax
from jax.experimental import pallas as pl
from jax.experimental.pallas import tpu as pltpu
from jax.sharding import PartitionSpec as P

MESH = pl.DeviceIdType.MESH
B = 64
HALF = 16
LANES = 128


def dft_table(points, groups):
    per_group = points // 2 // groups
    column = np.arange(points)
    group, rest = column // (2 * per_group), column % (2 * per_group)
    part, channel = rest // per_group, group * per_group + rest % per_group
    angle = (np.arange(points)[:, None] * channel[None, :] % points) * (2.0 * math.pi / points)
    value = np.where(part[None, :] == 0, np.cos(angle), -np.sin(angle)) / math.sqrt(points)
    return jnp.asarray(value.astype(np.float32)).astype(jnp.bfloat16)


def kernel(
    sizes,
    pairs_ref,
    x_hbm,
    proto_hbm,
    table_hbm,
    feed_hbm,
    keep_hbm,
    out_ref,
    x_ref,
    proto_ref,
    feed_ref,
    keep_ref,
    table_ref,
    place_ref,
    filt_ref,
    turn_out,
    turn_in,
    spill_one_out,
    spill_one_in,
    spill_two_out,
    spill_two_in,
    cat_ref,
    tile_out,
    tile_in,
    left_ref,
    right_ref,
    load_sem,
    turn_send,
    turn_recv,
    spill_send,
    spill_recv,
    tile_send,
    tile_recv,
):
    groups, n_tm, n_tile = sizes
    nodes = n_tm * n_tile
    me, tm, tile = lax.axis_index("freq"), lax.axis_index("tm"), lax.axis_index("tile")
    node = tm * n_tile + tile
    inputs, frames, points = x_hbm.shape

    def node_id(k):
        return (me, lax.div(k, n_tile), lax.rem(k, n_tile))

    loads = [
        pltpu.make_async_copy(src, dst, load_sem.at[i])
        for i, (src, dst) in enumerate(
            [
                (feed_hbm, feed_ref),
                (keep_hbm, keep_ref),
                (proto_hbm, proto_ref),
                (x_hbm, x_ref),
                (table_hbm, table_ref),
            ]
        )
    ]
    for load in loads:
        load.start()

    barrier = pltpu.get_barrier_semaphore()

    def greet_group(k, carry):
        pl.semaphore_signal(
            barrier, 1, device_id=(lax.rem(me + k, groups), tm, tile), device_id_type=MESH
        )
        return carry

    def greet_node(k, carry):
        pl.semaphore_signal(
            barrier, 1, device_id=node_id(lax.rem(node + k, nodes)), device_id_type=MESH
        )
        return carry

    before = lax.rem(node + nodes - 1, nodes)
    after = lax.rem(node + 1, nodes)

    def greet_before(k, carry):
        pl.semaphore_signal(
            barrier,
            1,
            device_id=(lax.rem(me + k, groups), lax.div(before, n_tile), lax.rem(before, n_tile)),
            device_id_type=MESH,
        )
        return carry

    lax.fori_loop(1, nodes, greet_node, 0)

    @pl.when(node > 0)
    def _():
        lax.fori_loop(0, groups, greet_before, 0)

    lax.fori_loop(1, groups, greet_group, 0)

    taps = proto_ref.shape[0]

    def column_of(row, first, size):
        lanes = lax.broadcasted_iota(jnp.int32, (size, LANES), 1)
        wanted = lax.broadcasted_iota(jnp.int32, (size, LANES), 0) + first
        picked = jnp.where(lanes == wanted, row.astype(jnp.float32), 0.0)
        return jnp.sum(picked, axis=1, keepdims=True)

    for load in loads[:4]:
        load.wait()
    per_row = LANES // inputs
    keep_row = keep_ref[pl.ds(lax.div(me, per_row), 1), :]
    keep = column_of(keep_row, lax.rem(me, per_row) * inputs, inputs)
    tiles_all = pairs_ref.shape[1]

    def build(k, carry):
        number = pairs_ref[lax.div(k, tiles_all), lax.rem(k, tiles_all)]
        row = feed_ref[pl.ds(lax.div(number, 2), 1), :]
        feeds = column_of(row, lax.rem(number, 2) * B, B).astype(jnp.int32)
        for q in range(2):
            place = lax.broadcasted_iota(jnp.int32, (1, groups * HALF), 1)
            source = lax.div(place, HALF) * inputs + lax.rem(place, HALF) + q * HALF
            place_ref[
                pl.ds(pl.multiple_of(k * B, B), B), q * groups * HALF : (q + 1) * groups * HALF
            ] = jnp.where(feeds == source, 1.0, 0.0).astype(jnp.bfloat16)
        return carry

    order = (3, 2, 6, 1, 0, 5, 4)

    def filter_columns(q, carry):
        cols = pl.ds(pl.multiple_of(q * 256, 256), 256)
        frame = [x_ref[:, k, cols].astype(jnp.float32) for k in range(frames)]
        for row, j in enumerate(order):
            total = None
            for lag in range(taps):
                if 0 <= j - lag < frames:
                    term = proto_ref[lag : lag + 1, cols] * frame[j - lag]
                    total = term if total is None else total + term
            filt_ref[row * inputs : (row + 1) * inputs, cols] = (total * keep).astype(
                jnp.bfloat16
            )
        return carry

    width = points // groups

    def channelize(q, carry):
        cols = pl.ds(pl.multiple_of(q * 256, 256), 256)
        y = jnp.dot(filt_ref[...], table_ref[:, cols], preferred_element_type=jnp.float32)

        def piece(first, size, b):
            return y[first : first + size, b * width : (b + 1) * width]

        def pair(row, b):
            pieces = [
                piece((row + f) * inputs + i * HALF, HALF, b) for i in range(2) for f in range(2)
            ]
            return jnp.concatenate(pieces, axis=1).astype(jnp.bfloat16)

        for b in range(256 // width):
            g = q * (256 // width) + b
            turn_out[0, g] = pair(0, b)
            turn_out[1, g] = pair(3, b)
            spill_two_out[g] = pair(5, b)
            eight = inputs // 4
            pieces = [piece(2 * inputs + i * eight, eight, b) for i in (1, 0, 3, 2)]
            spill_one_out[g] = jnp.concatenate(pieces, axis=1).astype(jnp.bfloat16)
        return carry

    spills = ((spill_one_out, spill_one_in), (spill_two_out, spill_two_in))

    def spill_copy(chunk, k):
        out, into = spills[chunk]
        peer = lax.rem(me + k, groups)
        return pltpu.make_async_remote_copy(
            src_ref=out.at[peer],
            dst_ref=into.at[me],
            send_sem=spill_send.at[chunk],
            recv_sem=spill_recv.at[chunk],
            device_id=(peer, lax.div(after, n_tile), lax.rem(after, n_tile)),
            device_id_type=MESH,
        )

    def spill_all(chunk):
        out, into = spills[chunk]
        return pltpu.make_async_remote_copy(
            src_ref=out,
            dst_ref=into,
            send_sem=spill_send.at[chunk],
            recv_sem=spill_recv.at[chunk],
            device_id=(me, lax.div(after, n_tile), lax.rem(after, n_tile)),
            device_id_type=MESH,
        )

    def send_spill(chunk):
        @pl.when(node < nodes - 1)
        def _():
            def go(k, carry):
                spill_copy(chunk, k).start()
                return carry

            lax.fori_loop(0, groups, go, 0)

    def wait_spill(chunk):
        into = spills[chunk][1]

        @pl.when(node == 0)
        def _():
            into[...] = jnp.zeros(into.shape, into.dtype)

        @pl.when(node > 0)
        def _():
            spill_all(chunk).wait_recv()

    def turn_copy(chunk, k):
        peer = lax.rem(me + k, groups)
        return pltpu.make_async_remote_copy(
            src_ref=turn_out.at[chunk, peer],
            dst_ref=turn_in.at[chunk, me],
            send_sem=turn_send.at[chunk],
            recv_sem=turn_recv.at[chunk],
            device_id=(peer, tm, tile),
            device_id_type=MESH,
        )

    def turn_all(chunk):
        return pltpu.make_async_remote_copy(
            src_ref=turn_out.at[chunk, pl.ds(0, groups - 1)],
            dst_ref=turn_in.at[chunk, pl.ds(0, groups - 1)],
            send_sem=turn_send.at[chunk],
            recv_sem=turn_recv.at[chunk],
            device_id=(lax.rem(me + 1, groups), tm, tile),
            device_id_type=MESH,
        )

    def send_turn(chunk):
        def go(k, carry):
            turn_copy(chunk, k).start()
            return carry

        lax.fori_loop(1, groups, go, 0)
        turn_in[chunk, me] = turn_out[chunk, me]

    def tile_copy(chunk, k):
        peer = lax.rem(node + k, nodes)
        return pltpu.make_async_remote_copy(
            src_ref=tile_out.at[chunk, peer],
            dst_ref=tile_in.at[chunk, node],
            send_sem=tile_send.at[chunk],
            recv_sem=tile_recv.at[chunk],
            device_id=node_id(peer),
            device_id_type=MESH,
        )

    def tile_all(chunk):
        return pltpu.make_async_remote_copy(
            src_ref=tile_out.at[chunk, pl.ds(0, nodes - 1)],
            dst_ref=tile_in.at[chunk, pl.ds(0, nodes - 1)],
            send_sem=tile_send.at[chunk],
            recv_sem=tile_recv.at[chunk],
            device_id=node_id(lax.rem(node + 1, nodes)),
            device_id_type=MESH,
        )

    rows_all = groups * HALF
    rows_node = tile_out.shape[2]
    per_step = 4

    def arrange(chunk):
        wait_spill(chunk)
        turn_all(chunk).wait_recv()
        block = turn_in[chunk].astype(jnp.float32)
        if chunk == 0:
            one = spill_one_in[...].astype(jnp.float32)
            lane = lax.broadcasted_iota(jnp.int32, one.shape, 2)
            odd = lax.rem(lax.div(lane, width), 2) == 1
            moved = jnp.where(odd, pltpu.roll(one, width, 2), 0.0)
            extra = jnp.concatenate([jnp.where(odd, one, 0.0), moved], axis=1)
        else:
            extra = spill_two_in[...].astype(jnp.float32)
        block = (block + extra).reshape(rows_all, LANES)
        cat_ref[0:rows_all] = block.astype(jnp.bfloat16)
        cat_ref[rows_all : 2 * rows_all] = pltpu.roll(block, B, 1).astype(jnp.bfloat16)
        low = lax.broadcasted_iota(jnp.int32, (per_step * rows_node, LANES), 1) < B

        def step(k, carry):
            size = per_step * rows_node
            first = pl.multiple_of(k * size, size)
            second = pl.multiple_of(nodes * rows_node + k * size, size)
            left = jnp.dot(
                place_ref[pl.ds(first, size), :], cat_ref[...], preferred_element_type=jnp.float32
            )
            right = jnp.dot(
                place_ref[pl.ds(second, size), :], cat_ref[...], preferred_element_type=jnp.float32
            )
            right = jnp.concatenate([right[:, B:], right[:, :B]], axis=1)
            both = jnp.where(low, left, right).astype(jnp.bfloat16)
            tile_out[chunk, pl.ds(k * per_step, per_step)] = both.reshape(
                per_step, rows_node, LANES
            )
            return carry

        lax.fori_loop(0, nodes // per_step, step, 0)

        def go(k, carry):
            tile_copy(chunk, k).start()
            return carry

        lax.fori_loop(1, nodes, go, 0)
        tile_in[chunk, node] = tile_out[chunk, node]

    lax.fori_loop(0, points // 256, filter_columns, 0)
    loads[4].wait()
    lax.fori_loop(0, points // 256, channelize, 0)
    expected = groups - 1 + nodes - 1 + jnp.where(node < nodes - 1, groups, 0)
    pl.semaphore_wait(barrier, expected)
    for chunk in range(2):
        send_spill(chunk)
        send_turn(chunk)
    lax.fori_loop(0, 2 * tiles_all, build, 0)
    arrange(0)
    arrange(1)

    tile_all(0).wait_recv()
    tile_all(1).wait_recv()
    lane = lax.broadcasted_iota(jnp.int32, (B, LANES), 1)
    low = lane < B
    channels = out_ref.shape[1]
    first_part = lax.rem(lane, 2 * channels) < channels
    shape = (channels, 1, nodes * LANES)
    own_lane = lax.rem(lax.broadcasted_iota(jnp.int32, shape, 2), channels)
    own_lane = own_lane == lax.broadcasted_iota(jnp.int32, shape, 0)
    own_lane = jnp.where(own_lane, 1.0, 0.0).astype(jnp.bfloat16)
    for t in range(out_ref.shape[0]):
        for k in range(nodes):
            one = tile_in[0, k, t * B : (t + 1) * B, :].astype(jnp.float32)
            two = tile_in[1, k, t * B : (t + 1) * B, :].astype(jnp.float32)
            one_turned = pltpu.roll(one, B, 1)
            two_turned = pltpu.roll(two, B, 1)
            left = jnp.where(low, one, two_turned)
            right = jnp.where(low, one_turned, two)
            cross = jnp.where(
                first_part, -pltpu.roll(right, LANES - channels, 1), pltpu.roll(right, channels, 1)
            )
            cols = slice(k * LANES, (k + 1) * LANES)
            left_ref[:, cols] = left.astype(jnp.bfloat16)
            right_ref[0:B, cols] = right.astype(jnp.bfloat16)
            right_ref[B : 2 * B, cols] = cross.astype(jnp.bfloat16)
        masked = (left_ref[...][None] * own_lane).reshape(channels * B, nodes * LANES)
        product = lax.dot_general(
            masked, right_ref[...], (((1,), (1,)), ((), ())), preferred_element_type=jnp.float32
        )
        out_ref[t] = (product * (1.0 / (frames * nodes))).reshape(channels, B, LANES)

    @pl.when(node < nodes - 1)
    def _():
        for chunk in range(2):
            spill_all(chunk).wait_send()

    for chunk in range(2):
        turn_all(chunk).wait_send()
        tile_all(chunk).wait_send()


def solution(mesh):
    groups, n_tm, n_tile = mesh.shape["freq"], mesh.shape["tm"], mesh.shape["tile"]
    nodes = n_tm * n_tile

    def shards(samples, prototype, feed_map, keep_mask, tile_pairs):
        taps = prototype.shape[0]
        inputs, frames, points = samples.shape
        total = inputs * groups
        tiles = tile_pairs.shape[0] // nodes
        channels = points // 2 // groups
        vmem = pl.BlockSpec(memory_space=pltpu.VMEM)
        bf = jnp.bfloat16
        body = lambda *refs: kernel((groups, n_tm, n_tile), *refs)
        return pl.pallas_call(
            body,
            out_shape=jax.ShapeDtypeStruct((tiles, channels, B, 2 * B), jnp.float32),
            in_specs=[pl.BlockSpec(memory_space=pltpu.SMEM)]
            + [pl.BlockSpec(memory_space=pltpu.HBM)] * 5,
            out_specs=vmem,
            scratch_shapes=[
                pltpu.VMEM((inputs, frames, points), bf),
                pltpu.VMEM((taps, points), jnp.float32),
                pltpu.VMEM((total // LANES, LANES), jnp.int32),
                pltpu.VMEM((total // LANES, LANES), jnp.int32),
                pltpu.VMEM((points, points), bf),
                pltpu.VMEM((total, total), bf),
                pltpu.VMEM((7 * inputs, points), bf),
                pltpu.VMEM((2, groups, HALF, LANES), bf),
                pltpu.VMEM((2, groups, HALF, LANES), bf),
                pltpu.VMEM((groups, HALF // 2, LANES), bf),
                pltpu.VMEM((groups, HALF // 2, LANES), bf),
                pltpu.VMEM((groups, HALF, LANES), bf),
                pltpu.VMEM((groups, HALF, LANES), bf),
                pltpu.VMEM((2 * groups * HALF, LANES), bf),
                pltpu.VMEM((2, nodes, tiles * B, LANES), bf),
                pltpu.VMEM((2, nodes, tiles * B, LANES), bf),
                pltpu.VMEM((B, nodes * LANES), bf),
                pltpu.VMEM((2 * B, nodes * LANES), bf),
                pltpu.SemaphoreType.DMA((5,)),
                pltpu.SemaphoreType.DMA((2,)),
                pltpu.SemaphoreType.DMA((2,)),
                pltpu.SemaphoreType.DMA((2,)),
                pltpu.SemaphoreType.DMA((2,)),
                pltpu.SemaphoreType.DMA((2,)),
                pltpu.SemaphoreType.DMA((2,)),
            ],
            compiler_params=pltpu.CompilerParams(
                collective_id=0, has_side_effects=True, vmem_limit_bytes=63 * 2**20
            ),
            cost_estimate=pl.CostEstimate(flops=4 * 10**9, bytes_accessed=10**7, transcendentals=0),
        )(
            tile_pairs.T,
            samples,
            prototype,
            dft_table(points, groups),
            feed_map.reshape(-1, LANES),
            keep_mask.reshape(-1, LANES),
        )

    return jax.shard_map(
        shards,
        mesh=mesh,
        in_specs=(P("freq", ("tm", "tile"), None), P(), P(), P(), P()),
        out_specs=P(("tm", "tile"), "freq", None, None),
        check_vma=False,
    )
```

time: 123 us -> 93.5 us (0.76)
  the two profiles are of different devices: /device:TPU:1 before, /device:TPU:18 now
where the time goes in v3:
time: 93.5 us; the launch traced here: 93.3 us
  Pallas kernels  91 us (97%)
  local copies, waits for them, and re-layouts  2.31 us (2%)
    pallas_call x1, Pallas kernels, shards(): pl.pallas_call(body, out_shape=jax.ShapeDtypeStruct((tiles, channels, B,...  91 us
    unnamed x1, local copies, waits for them, and re-layouts  2.31 us

profile of v3, /device:TPU:18, one launch (start us, length us, event | category | flops | bytes accessed | tf_op | source)
XLA Modules:
  0.0 93.3 jit_solution(11586577339659622157)
XLA Ops:
  0.0 91.0 %shard_map.64 = f32[2,16,64,128]{3,2,1,0:T(8,128)} custom-call(s32[2,16]{1,0:T(2,128)} %bitcast.5, bf16[32,4,2048]{2,1,0:T(4,128)(2,1)} %refs_1_.1, f32[4,2048]{1,0:T(4,128)} %refs_2_.1, bf16[2048,2048]{1,0:T(8,128)(2,1)} %constant.4.refs_3_, s32[16,128]{1,0:T(8,128)} %bitcast.3, s32[16,128]{1,0:T(8,128)} %bitcast.4), custom_call_target="tpu_custom_call" | custom-call | flops 4000000000 | bytes 10000000 | tf_op jit(solution)/shard_map/pallas_call | solution.py:396
  91.0 2.3 %copy.8 = f32[2,16,64,128]{3,2,1,0:T(8,128)} copy(f32[2,16,64,128]{3,2,1,0:T(8,128)} %shard_map.64) | data formatting | bytes 2097152

commit v4 on v3

--- a/solution.py
+++ b/solution.py
@@ -1,3 +1,4 @@
+import functools
 import math
 
 import jax
@@ -12,6 +13,7 @@
 B = 64
 HALF = 16
 LANES = 128
+STRIDE = 37
 
 
 def dft_table(points, groups):
@@ -21,7 +23,8 @@
     part, channel = rest // per_group, group * per_group + rest % per_group
     angle = (np.arange(points)[:, None] * channel[None, :] % points) * (2.0 * math.pi / points)
     value = np.where(part[None, :] == 0, np.cos(angle), -np.sin(angle)) / math.sqrt(points)
-    return jnp.asarray(value.astype(np.float32)).astype(jnp.bfloat16)
+    value = value.astype(np.float32).reshape(points, -1, 2 * LANES).transpose(1, 0, 2)
+    return jnp.asarray(value).astype(jnp.bfloat16)
 
 
 def kernel(
@@ -32,7 +35,7 @@
     table_hbm,
     feed_hbm,
     keep_hbm,
-    out_ref,
+    tile_in,
     x_ref,
     proto_ref,
     feed_ref,
@@ -48,10 +51,8 @@
     spill_two_in,
     cat_ref,
     tile_out,
-    tile_in,
-    left_ref,
-    right_ref,
     load_sem,
+    table_sem,
     turn_send,
     turn_recv,
     spill_send,
@@ -76,12 +77,22 @@
                 (keep_hbm, keep_ref),
                 (proto_hbm, proto_ref),
                 (x_hbm, x_ref),
-                (table_hbm, table_ref),
             ]
         )
     ]
     for load in loads:
         load.start()
+
+    blocks = table_ref.shape[0]
+
+    def table_load(q):
+        return pltpu.make_async_copy(table_hbm.at[q], table_ref.at[q], table_sem.at[q])
+
+    def load_table(q, carry):
+        table_load(q).start()
+        return carry
+
+    lax.fori_loop(0, blocks, load_table, 0)
 
     barrier = pltpu.get_barrier_semaphore()
 
@@ -125,7 +136,7 @@
         picked = jnp.where(lanes == wanted, row.astype(jnp.float32), 0.0)
         return jnp.sum(picked, axis=1, keepdims=True)
 
-    for load in loads[:4]:
+    for load in loads:
         load.wait()
     per_row = LANES // inputs
     keep_row = keep_ref[pl.ds(lax.div(me, per_row), 1), :]
@@ -163,8 +174,8 @@
     width = points // groups
 
     def channelize(q, carry):
-        cols = pl.ds(pl.multiple_of(q * 256, 256), 256)
-        y = jnp.dot(filt_ref[...], table_ref[:, cols], preferred_element_type=jnp.float32)
+        table_load(q).wait()
+        y = jnp.dot(filt_ref[...], table_ref[q], preferred_element_type=jnp.float32)
 
         def piece(first, size, b):
             return y[first : first + size, b * width : (b + 1) * width]
@@ -189,7 +200,7 @@
 
     def spill_copy(chunk, k):
         out, into = spills[chunk]
-        peer = lax.rem(me + k, groups)
+        peer = lax.rem(me + k * STRIDE, groups)
         return pltpu.make_async_remote_copy(
             src_ref=out.at[peer],
             dst_ref=into.at[me],
@@ -231,7 +242,7 @@
             spill_all(chunk).wait_recv()
 
     def turn_copy(chunk, k):
-        peer = lax.rem(me + k, groups)
+        peer = lax.rem(me + k * STRIDE, groups)
         return pltpu.make_async_remote_copy(
             src_ref=turn_out.at[chunk, peer],
             dst_ref=turn_in.at[chunk, me],
@@ -258,6 +269,15 @@
 
         lax.fori_loop(1, groups, go, 0)
         turn_in[chunk, me] = turn_out[chunk, me]
+
+    def wait_sent():
+        @pl.when(node < nodes - 1)
+        def _():
+            for chunk in range(2):
+                spill_all(chunk).wait_send()
+
+        for chunk in range(2):
+            turn_all(chunk).wait_send()
 
     def tile_copy(chunk, k):
         peer = lax.rem(node + k, nodes)
@@ -319,65 +339,69 @@
             return carry
 
         lax.fori_loop(0, nodes // per_step, step, 0)
-
-        def go(k, carry):
-            tile_copy(chunk, k).start()
+        if chunk == 0:
+            wait_sent()
+
+        def far(k, carry):
+            tile_copy(chunk, 2 * k + 1).start()
             return carry
 
-        lax.fori_loop(1, nodes, go, 0)
+        def near(k, carry):
+            tile_copy(chunk, 2 * k).start()
+            return carry
+
+        lax.fori_loop(0, nodes // 2, far, 0)
+        lax.fori_loop(1, nodes // 2, near, 0)
         tile_in[chunk, node] = tile_out[chunk, node]
 
     lax.fori_loop(0, points // 256, filter_columns, 0)
-    loads[4].wait()
-    lax.fori_loop(0, points // 256, channelize, 0)
+    lax.fori_loop(0, blocks, channelize, 0)
     expected = groups - 1 + nodes - 1 + jnp.where(node < nodes - 1, groups, 0)
     pl.semaphore_wait(barrier, expected)
-    for chunk in range(2):
-        send_spill(chunk)
-        send_turn(chunk)
+    send_spill(0)
+    send_spill(1)
+    send_turn(0)
+    send_turn(1)
     lax.fori_loop(0, 2 * tiles_all, build, 0)
     arrange(0)
     arrange(1)
 
     tile_all(0).wait_recv()
     tile_all(1).wait_recv()
+
+    tile_all(0).wait_send()
+    tile_all(1).wait_send()
+
+
+def correlate(scale, tile_in, out_ref, left_ref, right_ref):
     lane = lax.broadcasted_iota(jnp.int32, (B, LANES), 1)
     low = lane < B
     channels = out_ref.shape[1]
+    nodes = tile_in.shape[1]
     first_part = lax.rem(lane, 2 * channels) < channels
     shape = (channels, 1, nodes * LANES)
     own_lane = lax.rem(lax.broadcasted_iota(jnp.int32, shape, 2), channels)
     own_lane = own_lane == lax.broadcasted_iota(jnp.int32, shape, 0)
     own_lane = jnp.where(own_lane, 1.0, 0.0).astype(jnp.bfloat16)
-    for t in range(out_ref.shape[0]):
-        for k in range(nodes):
-            one = tile_in[0, k, t * B : (t + 1) * B, :].astype(jnp.float32)
-            two = tile_in[1, k, t * B : (t + 1) * B, :].astype(jnp.float32)
-            one_turned = pltpu.roll(one, B, 1)
-            two_turned = pltpu.roll(two, B, 1)
-            left = jnp.where(low, one, two_turned)
-            right = jnp.where(low, one_turned, two)
-            cross = jnp.where(
-                first_part, -pltpu.roll(right, LANES - channels, 1), pltpu.roll(right, channels, 1)
-            )
-            cols = slice(k * LANES, (k + 1) * LANES)
-            left_ref[:, cols] = left.astype(jnp.bfloat16)
-            right_ref[0:B, cols] = right.astype(jnp.bfloat16)
-            right_ref[B : 2 * B, cols] = cross.astype(jnp.bfloat16)
-        masked = (left_ref[...][None] * own_lane).reshape(channels * B, nodes * LANES)
-        product = lax.dot_general(
-            masked, right_ref[...], (((1,), (1,)), ((), ())), preferred_element_type=jnp.float32
-        )
-        out_ref[t] = (product * (1.0 / (frames * nodes))).reshape(channels, B, LANES)
-
-    @pl.when(node < nodes - 1)
-    def _():
-        for chunk in range(2):
-            spill_all(chunk).wait_send()
-
-    for chunk in range(2):
-        turn_all(chunk).wait_send()
-        tile_all(chunk).wait_send()
+    for k in range(nodes):
+        one = tile_in[0, k, :, :].astype(jnp.float32)
+        two = tile_in[1, k, :, :].astype(jnp.float32)
+        one_turned = pltpu.roll(one, B, 1)
+        two_turned = pltpu.roll(two, B, 1)
+        left = jnp.where(low, one, two_turned)
+        right = jnp.where(low, one_turned, two)
+        cross = jnp.where(
+            first_part, -pltpu.roll(right, LANES - channels, 1), pltpu.roll(right, channels, 1)
+        )
+        cols = slice(k * LANES, (k + 1) * LANES)
+        left_ref[:, cols] = left.astype(jnp.bfloat16)
+        right_ref[0:B, cols] = right.astype(jnp.bfloat16)
+        right_ref[B : 2 * B, cols] = cross.astype(jnp.bfloat16)
+    masked = (left_ref[...][None] * own_lane).reshape(channels * B, nodes * LANES)
+    product = lax.dot_general(
+        masked, right_ref[...], (((1,), (1,)), ((), ())), preferred_element_type=jnp.float32
+    )
+    out_ref[0] = (product * scale).reshape(channels, B, LANES)
 
 
 def solution(mesh):
@@ -390,12 +414,13 @@
         total = inputs * groups
         tiles = tile_pairs.shape[0] // nodes
         channels = points // 2 // groups
+        table = dft_table(points, groups)
         vmem = pl.BlockSpec(memory_space=pltpu.VMEM)
         bf = jnp.bfloat16
         body = lambda *refs: kernel((groups, n_tm, n_tile), *refs)
-        return pl.pallas_call(
+        field = pl.pallas_call(
             body,
-            out_shape=jax.ShapeDtypeStruct((tiles, channels, B, 2 * B), jnp.float32),
+            out_shape=jax.ShapeDtypeStruct((2, nodes, tiles * B, LANES), bf),
             in_specs=[pl.BlockSpec(memory_space=pltpu.SMEM)]
             + [pl.BlockSpec(memory_space=pltpu.HBM)] * 5,
             out_specs=vmem,
@@ -404,7 +429,7 @@
                 pltpu.VMEM((taps, points), jnp.float32),
                 pltpu.VMEM((total // LANES, LANES), jnp.int32),
                 pltpu.VMEM((total // LANES, LANES), jnp.int32),
-                pltpu.VMEM((points, points), bf),
+                pltpu.VMEM(table.shape, bf),
                 pltpu.VMEM((total, total), bf),
                 pltpu.VMEM((7 * inputs, points), bf),
                 pltpu.VMEM((2, groups, HALF, LANES), bf),
@@ -415,10 +440,8 @@
                 pltpu.VMEM((groups, HALF, LANES), bf),
                 pltpu.VMEM((2 * groups * HALF, LANES), bf),
                 pltpu.VMEM((2, nodes, tiles * B, LANES), bf),
-                pltpu.VMEM((2, nodes, tiles * B, LANES), bf),
-                pltpu.VMEM((B, nodes * LANES), bf),
-                pltpu.VMEM((2 * B, nodes * LANES), bf),
-                pltpu.SemaphoreType.DMA((5,)),
+                pltpu.SemaphoreType.DMA((4,)),
+                pltpu.SemaphoreType.DMA((table.shape[0],)),
                 pltpu.SemaphoreType.DMA((2,)),
                 pltpu.SemaphoreType.DMA((2,)),
                 pltpu.SemaphoreType.DMA((2,)),
@@ -434,10 +457,23 @@
             tile_pairs.T,
             samples,
             prototype,
-            dft_table(points, groups),
+            table,
             feed_map.reshape(-1, LANES),
             keep_mask.reshape(-1, LANES),
         )
+
+        return pl.pallas_call(
+            functools.partial(correlate, 1.0 / (frames * nodes)),
+            grid=(tiles,),
+            out_shape=jax.ShapeDtypeStruct((tiles, channels, B, 2 * B), jnp.float32),
+            in_specs=[pl.BlockSpec((2, nodes, B, LANES), lambda t: (0, 0, t, 0))],
+            out_specs=pl.BlockSpec((1, channels, B, 2 * B), lambda t: (t, 0, 0, 0)),
+            scratch_shapes=[
+                pltpu.VMEM((B, nodes * LANES), bf),
+                pltpu.VMEM((2 * B, nodes * LANES), bf),
+            ],
+            compiler_params=pltpu.CompilerParams(vmem_limit_bytes=32 * 2**20),
+        )(field)
 
     return jax.shard_map(
         shards,

time: 93.5 us -> 91.1 us (0.974)
  the two profiles are of different devices: /device:TPU:18 before, /device:TPU:1 now
where the time goes in v4:
time: 91.1 us; the launch traced here: 90.9 us
  Pallas kernels  89.9 us (99%)
  local copies, waits for them, and re-layouts  1.03 us (1%)
    pallas_call x1, Pallas kernels, shards(): pl.pallas_call(body, out_shape=jax.ShapeDtypeStruct((2, nodes, tiles * B,...  87.2 us
    pallas_call x1, Pallas kernels, shards(): pl.pallas_call(functools.partial(correlate, 1.0 / (frames * nodes)), grid...  2.66 us

profile of v4, /device:TPU:1, one launch (start us, length us, event | category | flops | bytes accessed | tf_op | source)
XLA Modules:
  0.0 90.9 jit_solution(9882017699016253821)
XLA Ops:
  0.0 87.2 %shard_map.64.tile_in = bf16[2,8,128,128]{3,2,1,0:T(8,128)(2,1)} custom-call(s32[2,16]{1,0:T(2,128)} %bitcast.5, bf16[32,4,2048]{2,1,0:T(4,128)(2,1)} %refs_1_.1, f32[4,2048]{1,0:T(4,128)} %refs_2_.1, bf16[8,2048,256]{2,1,0:T(8,128)(2,1)} %constant.4.refs_3_, s32[16,128]{1,0:T(8,128)} %bitcast.3, s32[16,128]{1,0:T(8,128)} %bitcast.4), custom_call_target="tpu_custom_call" | custom-call | flops 4000000000 | bytes 10000000 | tf_op jit(solution)/shard_map/pallas_call | solution.py:421
  87.2 0.0 copy-start
  87.2 1.0 %copy-done = bf16[2,8,128,128]{3,2,1,0:T(8,128)(2,1)S(1)} copy-done((bf16[2,8,128,128]{3,2,1,0:T(8,128)(2,1)S(1)}, bf16[2,8,128,128]{3,2,1,0:T(8,128)(2,1)}, u32[]{:S(2)}) %copy-start) | copy-done | bytes 524312
  88.3 2.7 %shard_map.65 = f32[2,16,64,128]{3,2,1,0:T(8,128)} custom-call(bf16[2,8,128,128]{3,2,1,0:T(8,128)(2,1)S(1)} %copy-done), custom_call_target="tpu_custom_call" | custom-call | tf_op jit(solution)/shard_map/pallas_call | solution.py:465
Async XLA Ops:
  87.2 1.0 %copy-start = (bf16[2,8,128,128]{3,2,1,0:T(8,128)(2,1)S(1)}, bf16[2,8,128,128]{3,2,1,0:T(8,128)(2,1)}, u32[]{:S(2)}) copy-start(bf16[2,8,128,128]{3,2,1,0:T(8,128)(2,1)} %shard_map.64.tile_in) | copy-start | bytes 1572868

commit v5 on v4

--- a/solution.py
+++ b/solution.py
@@ -155,12 +155,14 @@
             ] = jnp.where(feeds == source, 1.0, 0.0).astype(jnp.bfloat16)
         return carry
 
-    order = (3, 2, 6, 1, 0, 5, 4)
-
-    def filter_columns(q, carry):
+    order = (6, 5, 4, 3, 2, 1, 0)
+    spilled = taps - 1
+
+    def filter_columns(rows, q, carry):
         cols = pl.ds(pl.multiple_of(q * 256, 256), 256)
         frame = [x_ref[:, k, cols].astype(jnp.float32) for k in range(frames)]
-        for row, j in enumerate(order):
+        for row in rows:
+            j = order[row]
             total = None
             for lag in range(taps):
                 if 0 <= j - lag < frames:
@@ -171,29 +173,41 @@
             )
         return carry
 
+
     width = points // groups
-
-    def channelize(q, carry):
+    per_block = groups // blocks
+
+    def multiply(q, first, count):
+        rows = slice(first * inputs, (first + count) * inputs)
+        return jnp.dot(filt_ref[rows, :], table_ref[q], preferred_element_type=jnp.float32)
+
+    def pair(y, row, b):
+        pieces = [
+            y[(row + f) * inputs + i * HALF :, b * width : (b + 1) * width][:HALF]
+            for i in range(2)
+            for f in range(2)
+        ]
+        return jnp.concatenate(pieces, axis=1).astype(jnp.bfloat16)
+
+    def channelize_spilled(q, carry):
         table_load(q).wait()
-        y = jnp.dot(filt_ref[...], table_ref[q], preferred_element_type=jnp.float32)
-
-        def piece(first, size, b):
-            return y[first : first + size, b * width : (b + 1) * width]
-
-        def pair(row, b):
+        y = multiply(q, 0, spilled)
+        eight = inputs // 4
+        for b in range(per_block):
+            spill_two_out[q * per_block + b] = pair(y, 1, b)
             pieces = [
-                piece((row + f) * inputs + i * HALF, HALF, b) for i in range(2) for f in range(2)
+                y[i * eight : (i + 1) * eight, b * width : (b + 1) * width] for i in (1, 0, 3, 2)
             ]
-            return jnp.concatenate(pieces, axis=1).astype(jnp.bfloat16)
-
-        for b in range(256 // width):
-            g = q * (256 // width) + b
-            turn_out[0, g] = pair(0, b)
-            turn_out[1, g] = pair(3, b)
-            spill_two_out[g] = pair(5, b)
-            eight = inputs // 4
-            pieces = [piece(2 * inputs + i * eight, eight, b) for i in (1, 0, 3, 2)]
-            spill_one_out[g] = jnp.concatenate(pieces, axis=1).astype(jnp.bfloat16)
+            spill_one_out[q * per_block + b] = jnp.concatenate(pieces, axis=1).astype(
+                jnp.bfloat16
+            )
+        return carry
+
+    def channelize_own(q, carry):
+        y = multiply(q, spilled, frames)
+        for b in range(per_block):
+            turn_out[0, q * per_block + b] = pair(y, 0, b)
+            turn_out[1, q * per_block + b] = pair(y, 2, b)
         return carry
 
     spills = ((spill_one_out, spill_one_in), (spill_two_out, spill_two_in))
@@ -354,12 +368,15 @@
         lax.fori_loop(1, nodes // 2, near, 0)
         tile_in[chunk, node] = tile_out[chunk, node]
 
-    lax.fori_loop(0, points // 256, filter_columns, 0)
-    lax.fori_loop(0, blocks, channelize, 0)
+    first_rows, own_rows = range(spilled), range(spilled, spilled + frames)
+    lax.fori_loop(0, points // 256, functools.partial(filter_columns, first_rows), 0)
+    lax.fori_loop(0, blocks, channelize_spilled, 0)
     expected = groups - 1 + nodes - 1 + jnp.where(node < nodes - 1, groups, 0)
     pl.semaphore_wait(barrier, expected)
     send_spill(0)
     send_spill(1)
+    lax.fori_loop(0, points // 256, functools.partial(filter_columns, own_rows), 0)
+    lax.fori_loop(0, blocks, channelize_own, 0)
     send_turn(0)
     send_turn(1)
     lax.fori_loop(0, 2 * tiles_all, build, 0)

time: 91.1 us -> 97.9 us (1.075)
  the two profiles are of different devices: /device:TPU:1 before, /device:TPU:40 now
where the time goes in v5:
time: 97.9 us; the launch traced here: 97.7 us
  Pallas kernels  96.7 us (99%)
  local copies, waits for them, and re-layouts  1.03 us (1%)
    pallas_call x1, Pallas kernels, shards(): pl.pallas_call(body, out_shape=jax.ShapeDtypeStruct((2, nodes, tiles * B,...  94 us
    pallas_call x1, Pallas kernels, shards(): pl.pallas_call(functools.partial(correlate, 1.0 / (frames * nodes)), grid...  2.66 us

profile of v5, /device:TPU:40, one launch (start us, length us, event | category | flops | bytes accessed | tf_op | source)
XLA Modules:
  0.0 97.7 jit_solution(191326901331819610)
XLA Ops:
  0.0 94.0 %shard_map.64.tile_in = bf16[2,8,128,128]{3,2,1,0:T(8,128)(2,1)} custom-call(s32[2,16]{1,0:T(2,128)} %bitcast.5, bf16[32,4,2048]{2,1,0:T(4,128)(2,1)} %refs_1_.1, f32[4,2048]{1,0:T(4,128)} %refs_2_.1, bf16[8,2048,256]{2,1,0:T(8,128)(2,1)} %constant.4.refs_3_, s32[16,128]{1,0:T(8,128)} %bitcast.3, s32[16,128]{1,0:T(8,128)} %bitcast.4), custom_call_target="tpu_custom_call" | custom-call | flops 4000000000 | bytes 10000000 | tf_op jit(solution)/shard_map/pallas_call | solution.py:438
  94.0 0.0 copy-start
  94.0 1.0 %copy-done = bf16[2,8,128,128]{3,2,1,0:T(8,128)(2,1)S(1)} copy-done((bf16[2,8,128,128]{3,2,1,0:T(8,128)(2,1)S(1)}, bf16[2,8,128,128]{3,2,1,0:T(8,128)(2,1)}, u32[]{:S(2)}) %copy-start) | copy-done | bytes 524312
  95.1 2.7 %shard_map.65 = f32[2,16,64,128]{3,2,1,0:T(8,128)} custom-call(bf16[2,8,128,128]{3,2,1,0:T(8,128)(2,1)S(1)} %copy-done), custom_call_target="tpu_custom_call" | custom-call | tf_op jit(solution)/shard_map/pallas_call | solution.py:482
Async XLA Ops:
  94.0 1.0 %copy-start = (bf16[2,8,128,128]{3,2,1,0:T(8,128)(2,1)S(1)}, bf16[2,8,128,128]{3,2,1,0:T(8,128)(2,1)}, u32[]{:S(2)}) copy-start(bf16[2,8,128,128]{3,2,1,0:T(8,128)(2,1)} %shard_map.64.tile_in) | copy-start | bytes 1572868
